TPU v7x, 32 devices: a whole 2x2x4 slice. The times are simulated.
32 devices in a mesh: tier: 4 (over x, core), tile: 8 (over z, y).
Axes of the slice: x: 2, y: 2, z: 4, core: 2. Of those that a mesh axis runs over, the one named last changes fastest.
Arguments:
- starting_warmth_rise: float32 [32, 96, 1024], P('tile', 'tier'), may hold values from -3 to 8
- substance_per_cell: int32 [32, 96, 1024], P('tile', 'tier'), may hold values from 0 to 7
- material_transport_rates: float32 [2, 8], replicated, may hold values from 0.2 to 2
- patch_region_label: int32 [8, 8], P('tile'), may hold values from 0 to 15, as said below
- static_power_per_area: float32 [4, 16], replicated, may hold values from 0.5 to 4
- warming_power_factor: float32 [4, 16], replicated, may hold values from 0.2 to 0.8
- stacking_solve_operator: float32 [96, 96], replicated, may hold values from 0 to 1
Outputs:
- final_temperature: float32 [32, 96, 1024], P('tile', 'tier')
- block_power: float32 [4, 16], P('tier')
Inputs may be any that keep to these rules, and one draw needn't show every extreme that they name: `patch_region_label`: every block number names at least one tile.
All inputs are finite; a program needn't handle non-finite values.
Results may differ from a plain program's by a relative error of at most 0.0001.
Values sent between devices are 32-bit elements; how exact they have to be, the bound alone decides.
A program may use at most 64 MiB of HBM per device.

v0:
```python
import jax
import jax.numpy as jnp
from jax import lax
from jax.sharding import PartitionSpec as P

TILE_COLS = 128
STEPS = 2


LATERAL_RATE = 0.12
SOURCE_GAIN = 0.02


def extended(block, sides, width):
    for axis, dim in sides:
        count = lax.axis_size(axis)
        forward = [(i, i + 1) for i in range(count - 1)]
        backward = [(target, source) for source, target in forward]
        low = lax.ppermute(
            lax.slice_in_dim(block, block.shape[dim] - width, None, axis=dim), axis, forward
        )
        high = lax.ppermute(lax.slice_in_dim(block, 0, width, axis=dim), axis, backward)
        block = jnp.concatenate([low, block, high], axis=dim)
    return block


def pair_mean(cond_a, cond_b):
    return 2.0 * cond_a * cond_b / (cond_a + cond_b)


def lateral(padded, conduct):
    centre = padded[1:-1, :, 1:-1]
    sideways_coupling_rate = conduct[0, 1:-1, :, 1:-1]
    stacking_coupling_rate = conduct[1, 1:-1, :, 1:-1]
    flow_sum = pair_mean(sideways_coupling_rate, conduct[0, 2:, :, 1:-1]) * (
        padded[2:, :, 1:-1] - centre
    )
    flow_sum = flow_sum + pair_mean(sideways_coupling_rate, conduct[0, :-2, :, 1:-1]) * (
        padded[:-2, :, 1:-1] - centre
    )
    flow_sum = flow_sum + pair_mean(stacking_coupling_rate, conduct[1, 1:-1, :, 2:]) * (
        padded[1:-1, :, 2:] - centre
    )
    flow_sum = flow_sum + pair_mean(stacking_coupling_rate, conduct[1, 1:-1, :, :-2]) * (
        padded[1:-1, :, :-2] - centre
    )
    return centre + LATERAL_RATE * flow_sum


def exact_dot(left_op, right_op):
    return jnp.dot(
        left_op, right_op, precision=lax.Precision.HIGHEST, preferred_element_type=jnp.float32
    )


def lookup_codes(codes, material_transport_rates):
    sideways_coupling_rate = jnp.zeros(codes.shape, jnp.float32)
    stacking_coupling_rate = jnp.zeros(codes.shape, jnp.float32)
    for material in range(material_transport_rates.shape[1]):
        is_material = codes == material + 1
        sideways_coupling_rate = jnp.where(
            is_material, material_transport_rates[0, material], sideways_coupling_rate
        )
        stacking_coupling_rate = jnp.where(
            is_material, material_transport_rates[1, material], stacking_coupling_rate
        )
    return jnp.stack([sideways_coupling_rate, stacking_coupling_rate])


def tile_partials(active, tile_hot):
    mesh_height_cells, groups, col_count = active.shape
    quarter = col_count // TILE_COLS
    tile_sums = active.reshape(mesh_height_cells, groups, quarter, TILE_COLS).sum(axis=(0, 3))
    partial_value = exact_dot(tile_sums, tile_hot)
    counts = float(mesh_height_cells * TILE_COLS) * jnp.sum(tile_hot, axis=0)
    return (partial_value, counts)


def spread_power(block_power, tile_hot, mesh_height_cells):
    tile_power = exact_dot(block_power, tile_hot.T)
    groups, quarter = tile_power.shape
    cells = jnp.broadcast_to(
        tile_power[None, :, :, None], (mesh_height_cells, groups, quarter, TILE_COLS)
    )
    return cells.reshape(mesh_height_cells, groups, quarter * TILE_COLS)


def leak_tiers(active, tile_hot, static_power_per_area, warming_power_factor, tier_id):
    partial_value, counts = tile_partials(active, tile_hot)
    block_sum, block_count = lax.psum((partial_value[0], counts), "tile")
    base_row = lax.dynamic_slice_in_dim(static_power_per_area, tier_id, 1, 0)
    slope_row = lax.dynamic_slice_in_dim(warming_power_factor, tier_id, 1, 0)
    return base_row * jnp.exp(slope_row * block_sum[None, :] / block_count[None, :])


def shards(
    starting_warmth_rise,
    substance_per_cell,
    material_transport_rates,
    patch_region_label,
    static_power_per_area,
    warming_power_factor,
    stacking_solve_operator,
):
    mesh_height_cells, stacked_layer_number, lateral_width_cells = starting_warmth_rise.shape
    tier_id = lax.axis_index("tier")
    block_total = static_power_per_area.shape[1]
    codes = substance_per_cell + 1
    block_range = jnp.arange(block_total, dtype=jnp.int32)
    cond_pad = extended(lookup_codes(codes, material_transport_rates), (("tile", 1),), 1)
    cond_pad = jnp.pad(cond_pad, ((0, 0), (0, 0), (0, 0), (1, 1)))
    tile_hot = (patch_region_label[0][:, None] == block_range[None, :]).astype(jnp.float32)
    present_warming_state = starting_warmth_rise
    power_row = jnp.zeros((1, block_total), jnp.float32)
    for step_index in range(STEPS):
        padded = extended(present_warming_state, (("tile", 0),), 1)
        padded = jnp.pad(padded, ((0, 0), (0, 0), (1, 1)))
        power_row = leak_tiers(
            present_warming_state[:, ::stacked_layer_number, :],
            tile_hot,
            static_power_per_area,
            warming_power_factor,
            tier_id,
        )
        moved_field = lateral(padded, cond_pad)
        moved_field = moved_field.at[:, ::stacked_layer_number, :].add(
            SOURCE_GAIN * spread_power(power_row, tile_hot, mesh_height_cells)
        )
        applied = jnp.einsum(
            "lm,rmc->rlc",
            stacking_solve_operator,
            lax.all_to_all(moved_field, "tier", split_axis=2, concat_axis=1, tiled=True),
            precision=lax.Precision.HIGHEST,
        )
        present_warming_state = lax.all_to_all(
            applied, "tier", split_axis=1, concat_axis=2, tiled=True
        )
    return (present_warming_state, power_row)


def solution(mesh):
    in_specs = (
        P("tile", "tier", None),
        P("tile", "tier", None),
        P(),
        P("tile", None),
        P(),
        P(),
        P(),
    )
    out_specs = (P("tile", "tier", None), P("tier", None))
    return jax.shard_map(shards, mesh=mesh, in_specs=in_specs, out_specs=out_specs, check_vma=False)
```

profile of v0, /device:TPU:0, one launch (start us, length us, event | category | flops | bytes accessed | tf_op | source)
XLA Modules:
  0.0 142.5 jit_solution(3918848064363869905)
XLA Ops:
  0.6 1.0 fusion.41
  1.6 4.9 %collective-permute-start.3 = (f32[1,24,1024]{2,1,0:T(8,128)S(1)}, f32[1,24,1024]{2,1,0:T(8,128)S(1)}, u32[]{:S(2)}, u32[]{:S(2)}) collective-permute-start(f32[1,24,1024]{2,1,0:T(8,128)S(1)} %get-tuple-element.44), channel_id=1, source_target_pairs={{0,1},{1,2},{2,3},{3,4},{4,5},{5,6},{6,7},{8,9},{9,10},{10,11},{11... | collective-permute-start | bytes 294920 | tf_op jit(solution)/shard_map/ppermute | solution.py:19
  6.5 1.3 collective-permute-start.1
  7.8 2.0 %fusion.42 = (f32[1,1]{1,0:T(1,128)}, f32[1,1]{1,0:T(1,128)}, f32[1,1]{1,0:T(1,128)}, f32[1,1]{1,0:T(1,128)}, f32[1,1]{1,0:T(1,128)}, /*index=5*/f32[1,1]{1,0:T(...) fusion(f32[2,8]{1,0:T(2,128)} %param.13), kind=kLoop, calls=%fused_computation.105 | loop fusion | bytes 128 | tf_op jit(solution)/shard_map/slice | solution.py:62
  9.8 6.6 %select_select_fusion = (f32[4,24,1024]{2,1,0:T(8,128)S(1)}, pred[4,24,1024]{2,1,0:T(8,128)(4,1)S(1)}, pred[4,24,1024]{2,1,0:T(8,128)(4,1)S(1)}, pred[4,24,1024]...) fusion(f32[]{:T(128)} %bitcast.16, f32[]{:T(128)} %bitcast.15, ...), kind=kLoop, calls=%fused_computation.62 | loop fusion | flops 1671168 | bytes 1572896 | tf_op jit(solution)/shard_map/jit(_where)/select_n | solution.py:64
  16.4 5.4 %select_select_fusion.1 = f32[4,24,1024]{2,1,0:T(8,128)S(1)} fusion(pred[4,24,1024]{2,1,0:T(8,128)(4,1)S(1)} %get-tuple-element.39, pred[4,24,1024]{2,1,0:T(8,128)(4,1)S(1)} %get-tuple-element.38, pred[4,24,1024]{2,1,0:T(8,128)(4,1)S(1)} %get-tuple-element.37, pred[4,24,1024]{2,1,0:T(8,128)(4,1)S(1)} %get-tuple-element.36, ...), kind=kLoop, calls=%fused_computation.63 | loop fusion | flops 786432 | bytes 1179680 | tf_op jit(solution)/shard_map/jit(_where)/select_n | solution.py:61
  21.8 4.6 %collective-permute-start.2 = (f32[2,1,24,1024]{3,2,1,0:T(8,128)S(1)}, f32[2,1,24,1024]{3,2,1,0:T(8,128)S(1)}, u32[]{:S(2)}, u32[]{:S(2)}) collective-permute-start(f32[2,1,24,1024]{3,2,1,0:T(8,128)S(1)} %get-tuple-element.40), channel_id=1, source_target_pairs={{0,1},{1,2},{2,3},{3,4},{4,5},{5,6},{6,7},{8,9},{9,10},{10,11},{11... | collective-permute-start | bytes 589832 | tf_op jit(solution)/shard_map/ppermute | solution.py:19
  26.3 1.3 collective-permute-start
  28.1 22.8 %all-reduce.3 = (f32[1,16]{1,0:T(1,128)S(1)}, f32[1,16]{1,0:T(1,128)S(1)}) all-reduce(f32[1,16]{1,0:T(1,128)S(1)} %multiply_bitcast_fusion.2, f32[1,16]{1,0:T(1,128)S(1)} %fusion.31), channel_id=1, replica_groups=mesh['tier'=4,'tile'=8] {'tile'}, use_global_device_ids=true, to_apply=%region_4.5 | all-reduce | flops 32 | bytes 256 | tf_op jit(solution)/shard_map/psum | solution.py:90
  51.9 1.2 fusion.18
  53.3 0.9 copy.88
  54.1 2.9 %reshape.124 = f32[4,1,24576]{2,1,0:T(1,128)S(1)} reshape(f32[1024,4,24]{2,1,0:T(4,128)S(1)} %bitcast.115) | data formatting | bytes 786432
  57.0 10.0 %all_to_all.72 = f32[4,1,24576]{2,1,0:T(1,128)S(1)} all-to-all(f32[4,1,24576]{2,1,0:T(1,128)S(1)} %reshape.124), channel_id=1, replica_groups=mesh['tier'=4,'tile'=8] {'tier'}, dimensions={0} | all-to-all | bytes 786432 | tf_op jit(solution)/shard_map/all_to_all | solution.py:132
  67.0 0.5 broadcast.157
  67.5 1.7 %reduce.10 = f32[4,24576]{1,0:T(4,128)S(1)} reduce(f32[4,1,24576]{2,1,0:T(1,128)S(1)} %all_to_all.72, f32[]{:T(128)} %broadcast.157), dimensions={1}, to_apply=%all_to_all.52.reduce_sub_computation | reduce | bytes 786436 | tf_op jit(solution)/shard_map/all_to_all | solution.py:132
  69.3 2.8 %reshape.125 = f32[1024,4,24]{2,1,0:T(4,128)S(1)} reshape(f32[4,24576]{1,0:T(4,128)S(1)} %reduce.10) | data formatting | bytes 786432
  72.1 0.8 copy.89
  73.6 9.8 %all_to_all.73 = f32[4,96,256]{2,0,1:T(4,128)S(1)} all-to-all(f32[4,96,256]{2,0,1:T(4,128)S(1)} %copy.90), channel_id=1, replica_groups=mesh['tier'=4,'tile'=8] {'tier'}, dimensions={1} | all-to-all | bytes 786432 | tf_op jit(solution)/shard_map/all_to_all | solution.py:135
  84.3 17.1 %psum.26 = f32[1,16]{1,0:T(1,128)S(1)} all-reduce(f32[1,16]{1,0:T(1,128)S(1)} %fusion.30), channel_id=1, replica_groups=mesh['tier'=4,'tile'=8] {'tile'}, use_global_device_ids=true, to_apply=%region_7.8 | all-reduce | flops 16 | bytes 128 | tf_op jit(solution)/shard_map/psum | solution.py:90
  101.7 1.3 collective-permute-start.4
  103.0 4.6 %collective-permute-start.5 = (f32[1,24,1024]{2,1,0:T(8,128)S(1)}, f32[1,24,1024]{2,1,0:T(8,128)S(1)}, u32[]{:S(2)}, u32[]{:S(2)}) collective-permute-start(f32[1,24,1024]{2,1,0:T(8,128)S(1)} %slice.222), channel_id=1, source_target_pairs={{0,1},{1,2},{2,3},{3,4},{4,5},{5,6},{6,7},{8,9},{9,10},{10,11},{11... | collective-permute-start | bytes 294920 | tf_op jit(solution)/shard_map/ppermute | solution.py:19
  107.7 0.6 collective-permute-done.4
  108.3 1.5 %collective-permute-done.5 = f32[1,24,1024]{2,1,0:T(8,128)S(1)} collective-permute-done((f32[1,24,1024]{2,1,0:T(8,128)S(1)}, f32[1,24,1024]{2,1,0:T(8,128)S(1)}, u32[]{:S(2)}, u32[]{:S(2)}) %collective-permute-start.5) | collective-permute-done | bytes 98336 | tf_op jit(solution)/shard_map/ppermute | solution.py:19
  110.0 1.4 fusion.7
  111.8 0.9 copy.92
  112.7 2.9 %reshape.126 = f32[4,1,24576]{2,1,0:T(1,128)S(1)} reshape(f32[1024,4,24]{2,1,0:T(4,128)S(1)} %bitcast.117) | data formatting | bytes 786432
  115.6 9.8 %all_to_all.74 = f32[4,1,24576]{2,1,0:T(1,128)S(1)} all-to-all(f32[4,1,24576]{2,1,0:T(1,128)S(1)} %reshape.126), channel_id=1, replica_groups=mesh['tier'=4,'tile'=8] {'tier'}, dimensions={0} | all-to-all | bytes 786432 | tf_op jit(solution)/shard_map/all_to_all | solution.py:132
  125.4 1.7 %reduce.11 = f32[4,24576]{1,0:T(4,128)S(1)} reduce(f32[4,1,24576]{2,1,0:T(1,128)S(1)} %all_to_all.74, f32[]{:T(128)} %broadcast.157), dimensions={1}, to_apply=%all_to_all.60.reduce_sub_computation | reduce | bytes 786436 | tf_op jit(solution)/shard_map/all_to_all | solution.py:132
  127.1 2.8 %reshape.127 = f32[1024,4,24]{2,1,0:T(4,128)S(1)} reshape(f32[4,24576]{1,0:T(4,128)S(1)} %reduce.11) | data formatting | bytes 786432
  129.9 0.8 copy.93
  131.4 9.8 %all_to_all.75 = f32[4,96,256]{2,0,1:T(4,128)S(1)} all-to-all(f32[4,96,256]{2,0,1:T(4,128)S(1)} %copy.94), channel_id=1, replica_groups=mesh['tier'=4,'tile'=8] {'tier'}, dimensions={1} | all-to-all | bytes 786432 | tf_op jit(solution)/shard_map/all_to_all | solution.py:135
  141.5 0.9 all_to_all.67
  (51 shorter events, 5.1 us)
Async XLA Ops:
  0.6 72.2 %copy-start = (f32[96,96]{1,0:T(8,128)S(1)}, f32[96,96]{1,0:T(8,128)}, u32[]{:S(2)}) copy-start(f32[96,96]{1,0:T(8,128)} %param.17) | copy-start | bytes 110596
  1.6 49.5 %collective-permute-start.3 = (f32[1,24,1024]{2,1,0:T(8,128)S(1)}, f32[1,24,1024]{2,1,0:T(8,128)S(1)}, u32[]{:S(2)}, u32[]{:S(2)}) collective-permute-start(f32[1,24,1024]{2,1,0:T(8,128)S(1)} %get-tuple-element.44), channel_id=1, source_target_pairs={{0,1},{1,2},{2,3},{3,4},{4,5},{5,6},{6,7},{8,9},{9,10},{10,11},{11... | collective-permute-start | bytes 294920 | tf_op jit(solution)/shard_map/ppermute | solution.py:19
  6.5 44.7 %collective-permute-start.1 = (f32[1,24,1024]{2,1,0:T(8,128)S(1)}, f32[1,24,1024]{2,1,0:T(8,128)S(1)}, u32[]{:S(2)}, u32[]{:S(2)}) collective-permute-start(f32[1,24,1024]{2,1,0:T(8,128)S(1)} %get-tuple-element.45), channel_id=1, source_target_pairs={{1,0},{2,1},{3,2},{4,3},{5,4},{6,5},{7,6},{9,8},{10,9},{11,10},{12... | collective-permute-start | bytes 294920 | tf_op jit(solution)/shard_map/ppermute | solution.py:22
  16.3 11.3 %copy-start.3 = (f32[4,24,1024]{2,1,0:T(8,128)S(1)}, f32[4,24,1024]{2,1,0:T(8,128)}, u32[]{:S(2)}) copy-start(f32[4,24,1024]{2,1,0:T(8,128)} %param.11) | copy-start | bytes 1179652
  16.3 11.3 %copy-start.7 = (s32[1,8]{1,0:T(1,128)S(1)}, s32[1,8]{1,0:T(1,128)}, u32[]{:S(2)}) copy-start(s32[1,8]{1,0:T(1,128)} %param.14) | copy-start | bytes 100
  16.4 34.5 %copy-start.5 = (f32[4,16]{1,0:T(4,128)S(1)}, f32[4,16]{1,0:T(4,128)}, u32[]{:S(2)}) copy-start(f32[4,16]{1,0:T(4,128)} %param.15) | copy-start | bytes 772
  16.4 34.5 %copy-start.6 = (f32[4,16]{1,0:T(4,128)S(1)}, f32[4,16]{1,0:T(4,128)}, u32[]{:S(2)}) copy-start(f32[4,16]{1,0:T(4,128)} %param.16) | copy-start | bytes 772
  21.8 29.6 %collective-permute-start.2 = (f32[2,1,24,1024]{3,2,1,0:T(8,128)S(1)}, f32[2,1,24,1024]{3,2,1,0:T(8,128)S(1)}, u32[]{:S(2)}, u32[]{:S(2)}) collective-permute-start(f32[2,1,24,1024]{3,2,1,0:T(8,128)S(1)} %get-tuple-element.40), channel_id=1, source_target_pairs={{0,1},{1,2},{2,3},{3,4},{4,5},{5,6},{6,7},{8,9},{9,10},{10,11},{11... | collective-permute-start | bytes 589832 | tf_op jit(solution)/shard_map/ppermute | solution.py:19
  26.3 25.1 %collective-permute-start = (f32[2,1,24,1024]{3,2,1,0:T(8,128)S(1)}, f32[2,1,24,1024]{3,2,1,0:T(8,128)S(1)}, u32[]{:S(2)}, u32[]{:S(2)}) collective-permute-start(f32[2,1,24,1024]{3,2,1,0:T(8,128)S(1)} %get-tuple-element.41), channel_id=1, source_target_pairs={{1,0},{2,1},{3,2},{4,3},{5,4},{6,5},{7,6},{9,8},{10,9},{11,10},{12... | collective-permute-start | bytes 589832 | tf_op jit(solution)/shard_map/ppermute | solution.py:22
  51.8 1.3 copy-start.1
  83.7 26.3 %copy-start.2 = (f32[2,6,24,1026]{3,2,1,0:T(8,128)S(1)}, f32[2,6,24,1026]{3,2,1,0:T(8,128)}, u32[]{:S(2)}) copy-start(f32[2,6,24,1026]{3,2,1,0:T(8,128)} %copy-done.1) | copy-start | bytes 3545860
  101.5 10.0 %copy-start.4 = (f32[1,16]{1,0:T(1,128)}, f32[1,16]{1,0:T(1,128)S(1)}, u32[]{:S(2)}) copy-start(f32[1,16]{1,0:T(1,128)S(1)} %exponential_multiply_fusion) | copy-start | bytes 196
  101.7 6.5 %collective-permute-start.4 = (f32[1,24,1024]{2,1,0:T(8,128)S(1)}, f32[1,24,1024]{2,1,0:T(8,128)S(1)}, u32[]{:S(2)}, u32[]{:S(2)}) collective-permute-start(f32[1,24,1024]{2,1,0:T(8,128)S(1)} %slice.219), channel_id=1, source_target_pairs={{1,0},{2,1},{3,2},{4,3},{5,4},{6,5},{7,6},{9,8},{10,9},{11,10},{12... | collective-permute-start | bytes 294920 | tf_op jit(solution)/shard_map/ppermute | solution.py:22
  103.0 6.8 %collective-permute-start.5 = (f32[1,24,1024]{2,1,0:T(8,128)S(1)}, f32[1,24,1024]{2,1,0:T(8,128)S(1)}, u32[]{:S(2)}, u32[]{:S(2)}) collective-permute-start(f32[1,24,1024]{2,1,0:T(8,128)S(1)} %slice.222), channel_id=1, source_target_pairs={{0,1},{1,2},{2,3},{3,4},{4,5},{5,6},{6,7},{8,9},{9,10},{10,11},{11... | collective-permute-start | bytes 294920 | tf_op jit(solution)/shard_map/ppermute | solution.py:19
where the time goes:
time: 145 us; the launch traced here: 142 us
  blocking collectives  79.4 us (55%)
  local copies, waits for them, and re-layouts  21 us (14%)
  other arithmetic  19.3 us (13%)
  starting transfers between devices  17.9 us (12%)
  waiting for transfers between devices  2.13 us (1%)
  matrix products  1.71 us (1%)
    psum x2, blocking collectives, leak_tiers(): block_sum, block_count = lax.psum((partial_value[0], counts), 'tile')  39.9 us
    all_to_all x2, blocking collectives, shards(): lax.all_to_all(moved_field, 'tier', split_axis=2, concat_axis=1, tiled=True)  19.8 us
    all_to_all x2, blocking collectives, shards(): lax.all_to_all(applied, 'tier', split_axis=1, concat_axis=2, tiled=True)  19.7 us
    ppermute x3, starting transfers between devices, extended(): lax.ppermute(lax.slice_in_dim(block, block.shape[dim] - width, None, axis...  14 us
    unnamed x20, local copies, waits for them, and re-layouts  11.4 us
    select_n x1, other arithmetic, lookup_codes(): jnp.where(is_material, material_transport_rates[1, material], stacking_co...  6.55 us
    select_n x1, other arithmetic, lookup_codes(): jnp.where(is_material, material_transport_rates[0, material], sideways_co...  5.36 us
    ppermute x3, starting transfers between devices, extended(): lax.ppermute(lax.slice_in_dim(block, 0, width, axis=dim), axis, backward)  3.88 us
  transfers between devices with their start and end apart: 6, of which 2 were waited for; matrix products, arithmetic and copies ran while one was open for 10% of the time, Pallas kernels for 0%

commit v1 on v0

v1 whole, which is shorter than its diff:
```python
import functools

import jax
import jax.numpy as jnp
from jax import lax
from jax.experimental import pallas as pl
from jax.experimental.pallas import tpu as pltpu
from jax.sharding import PartitionSpec as P

TILE_COLS = 128
LATERAL_RATE = 0.12
SOURCE_GAIN = 0.02
MESH = pl.DeviceIdType.MESH


def face(a, b):
    return (2.0 * LATERAL_RATE) * a * b / (a + b)


def solve(op, x):
    return jnp.dot(op, x, precision=lax.Precision.HIGHEST, preferred_element_type=jnp.float32)


def kernel(
    ntier, ntile, nblk,
    t_in, m_in, rates, labels, stat, fac, a_in,
    out, pw_out,
    halo_t, halo_m, mv, e_mat, e_mv, col_m, col_me, col_mh, col, col_e, t1, halo_1, mv2, res,
    cx, cy, cl, p1, p2a, p2b,
    s_halo, r_halo, s_a2a, r_a2a, s_mat, r_mat, s_me, r_me, s_e, r_e, s_out, r_out,
    s_p1, r_p1, s_pa, r_pa, s_pb, r_pb,
):
    tier = lax.axis_index("tier")
    tile = lax.axis_index("tile")
    rows, lev, width = t_in.shape
    cols = width // ntier
    quarter = cols // TILE_COLS
    levels = lev * ntier
    nmat = rates.shape[1]
    order = [r for r in range(1, rows - 1)] + [0, rows - 1]

    def tier_at(k):
        return lax.rem(tier + k, ntier)

    def tile_at(k):
        return lax.rem(tile + k, ntile)

    def window(index):
        return pl.ds(pl.multiple_of(index * cols, TILE_COLS), cols)

    def group(index):
        return pl.ds(pl.multiple_of(index * lev, 8), lev)

    barrier = pltpu.get_barrier_semaphore()
    for k in range(1, ntier):
        pl.semaphore_signal(barrier, inc=1, device_id={"tier": tier_at(k)}, device_id_type=MESH)

    def greet(k, carry):
        pl.semaphore_signal(barrier, inc=1, device_id={"tile": tile_at(k)}, device_id_type=MESH)
        return carry

    lax.fori_loop(1, ntile, greet, 0)

    def lookup(codes, axes):
        outs = [jnp.full(codes.shape, rates[a, 0], jnp.float32) for a in axes]
        for m in range(1, nmat):
            hit = codes == m
            outs = [jnp.where(hit, rates[a, m], o) for a, o in zip(axes, outs)]
        return outs

    lane = lax.broadcasted_iota(jnp.int32, (lev, TILE_COLS), 1)
    pair = lane >> 1

    def pack_edges(src, dst):
        for d in range(ntier):
            low = max(d * cols - TILE_COLS, 0)
            high = min((d + 1) * cols, width - TILE_COLS)
            acc = jnp.zeros((lev, TILE_COLS), src.dtype)
            for r in range(rows):
                both = jnp.where(
                    lane == TILE_COLS - 1,
                    src[r, :, low : low + TILE_COLS],
                    src[r, :, high : high + TILE_COLS],
                )
                acc = jnp.where(pair == r, pltpu.roll(both, 2 * r + 1, 1), acc)
            dst[d] = acc

    blk1 = lax.broadcasted_iota(jnp.int32, (1, nblk), 1)
    blkn = lax.broadcasted_iota(jnp.int32, (ntier, nblk), 1)

    sums = jnp.zeros((1, nblk), jnp.float32)
    areas = jnp.zeros((1, nblk), jnp.float32)
    active = t_in[0, 0:1, :]
    for r in range(1, rows):
        active = active + t_in[r, 0:1, :]
    for j in range(width // TILE_COLS):
        part = jnp.sum(active[:, j * TILE_COLS : (j + 1) * TILE_COLS], axis=1, keepdims=True)
        hit = blk1 == labels[0, j]
        sums = sums + jnp.where(hit, part, 0.0)
        areas = areas + jnp.where(hit, float(rows * TILE_COLS), 0.0)
    p1[0] = jnp.zeros(p1.shape[1:], jnp.float32)
    p1[0, 0:1, 0:nblk] = sums
    p1[0, 1:2, 0:nblk] = areas
    pack_edges(m_in, e_mat)

    pl.semaphore_wait(barrier, ntier - 1 + ntile - 1)

    def share(buf, s_sem, r_sem):
        def send(k, carry):
            pltpu.make_async_remote_copy(
                src_ref=buf.at[0], dst_ref=buf.at[k], send_sem=s_sem, recv_sem=r_sem,
                device_id={"tile": tile_at(k)}, device_id_type=MESH,
            ).start()
            return carry

        lax.fori_loop(1, ntile, send, 0)

    def shared(buf, r_sem):
        rest = buf.at[pl.ds(1, ntile - 1)]
        pltpu.make_async_copy(rest, rest, r_sem).wait()

    def total(buf):
        return lax.fori_loop(1, ntile, lambda k, acc: acc + buf[k], buf[0])

    share(p1, s_p1, r_p1)

    def halo_copies(low_src, high_src, dst, which):
        down = pltpu.make_async_remote_copy(
            src_ref=low_src, dst_ref=dst.at[1],
            send_sem=s_halo.at[which, 0], recv_sem=r_halo.at[which, 1],
            device_id={"tile": lax.max(tile - 1, 0)}, device_id_type=MESH,
        )
        up = pltpu.make_async_remote_copy(
            src_ref=high_src, dst_ref=dst.at[0],
            send_sem=s_halo.at[which, 1], recv_sem=r_halo.at[which, 0],
            device_id={"tile": lax.min(tile + 1, ntile - 1)}, device_id_type=MESH,
        )
        return down, up

    has_low = tile > 0
    has_high = tile < ntile - 1

    def halo_start(copies):
        pl.when(has_low)(lambda: copies[0].start())
        pl.when(has_high)(lambda: copies[1].start())

    def halo_recv(copies):
        pl.when(has_low)(lambda: copies[1].wait_recv())
        pl.when(has_high)(lambda: copies[0].wait_recv())

    def halo_sent(copies):
        pl.when(has_low)(lambda: copies[0].wait_send())
        pl.when(has_high)(lambda: copies[1].wait_send())

    @pl.when(jnp.logical_not(has_low))
    def _():
        halo_t[0] = jnp.zeros(halo_t.shape[1:], jnp.float32)
        halo_m[0] = jnp.zeros(halo_m.shape[1:], jnp.int32)
        halo_1[0] = jnp.zeros(halo_1.shape[1:], jnp.float32)
        col_mh[0] = jnp.zeros(col_mh.shape[1:], jnp.int32)

    @pl.when(jnp.logical_not(has_high))
    def _():
        halo_t[1] = jnp.zeros(halo_t.shape[1:], jnp.float32)
        halo_m[1] = jnp.zeros(halo_m.shape[1:], jnp.int32)
        halo_1[1] = jnp.zeros(halo_1.shape[1:], jnp.float32)
        col_mh[1] = jnp.zeros(col_mh.shape[1:], jnp.int32)

    temp_halo = halo_copies(t_in.at[0], t_in.at[rows - 1], halo_t, 0)
    mat_halo = halo_copies(m_in.at[0], m_in.at[rows - 1], halo_m, 1)
    halo_start(temp_halo)
    halo_start(mat_halo)

    def to_tier(src, dst, s_sem, r_sem, k):
        return pltpu.make_async_remote_copy(
            src_ref=src, dst_ref=dst, send_sem=s_sem, recv_sem=r_sem,
            device_id={"tier": tier_at(k)}, device_id_type=MESH,
        )

    def mat_copy(k, receive):
        src = tier_at(ntier - k) if receive else tier
        return to_tier(
            m_in.at[:, :, window(tier_at(k))], col_m.at[:, group(src), :],
            s_mat.at[k], r_mat.at[k], k,
        )

    def edge_copy(k, receive, src_ref, dst_ref, s_sem, r_sem):
        src = tier_at(ntier - k) if receive else tier
        return to_tier(
            src_ref.at[tier_at(k)], dst_ref.at[group(src), :], s_sem.at[k], r_sem.at[k], k
        )

    def row_copy(r, k, receive):
        src = tier_at(ntier - k) if receive else tier
        return to_tier(
            mv.at[r, :, window(tier_at(k))], col.at[r, group(src), :],
            s_a2a.at[r, k], r_a2a.at[r, k], k,
        )

    def out_copy(r, k, receive):
        src = tier_at(ntier - k) if receive else tier
        return to_tier(
            res.at[r, group(tier_at(k)), :], out.at[r, :, window(src)],
            s_out.at[r, k], r_out.at[r, k], k,
        )

    for k in range(1, ntier):
        mat_copy(k, False).start()
        edge_copy(k, False, e_mat, col_me, s_me, r_me).start()
    col_m[:, group(tier), :] = m_in[:, :, window(tier)]
    col_me[group(tier), :] = e_mat[tier]

    wide = lax.broadcasted_iota(jnp.int32, (lev, width), 1)
    before = None
    for r in range(rows):
        kx, ky = lookup(m_in[r], (0, 1))
        here = t_in[r]
        flux = jnp.where(
            wide == width - 1, 0.0, face(ky, pltpu.roll(ky, width - 1, 1))
        ) * (pltpu.roll(here, width - 1, 1) - here)
        mv[r] = here + (flux - pltpu.roll(flux, 1, 1))
        if r > 0:
            flow = face(before, kx) * (here - t_in[r - 1])
            mv[r] -= flow
            mv[r - 1] += flow
        before = kx

    shared(p1, r_p1)
    whole = total(p1)
    count = whole[1:2, 0:nblk]
    power = stat[pl.ds(tier, 1), :] * jnp.exp(
        fac[pl.ds(tier, 1), :] * whole[0:1, 0:nblk] / count
    )
    gain = []
    for j in range(width // TILE_COLS):
        mine = jnp.sum(jnp.where(blk1 == labels[0, j], power, 0.0), axis=1, keepdims=True)
        gain.append(jnp.broadcast_to(SOURCE_GAIN * mine, (1, TILE_COLS)))
    gain = jnp.concatenate(gain, axis=1)
    for r in range(rows):
        mv[r, 0:1, :] += gain

    for r in order[:-2]:
        for k in range(1, ntier):
            row_copy(r, k, False).start()
        col[r, group(tier), :] = mv[r, :, window(tier)]

    halo_recv(temp_halo)
    halo_recv(mat_halo)
    for r, side, inside in ((0, 0, has_low), (rows - 1, 1, has_high)):
        (own,) = lookup(m_in[r], (0,))
        (other,) = lookup(halo_m[side], (0,))
        other = jnp.where(inside, other, 0.0)
        mv[r] += face(own, other) * (halo_t[side] - t_in[r])
        for k in range(1, ntier):
            row_copy(r, k, False).start()
        col[r, group(tier), :] = mv[r, :, window(tier)]
    pack_edges(mv, e_mv)
    for k in range(1, ntier):
        edge_copy(k, False, e_mv, col_e, s_e, r_e).start()
    col_e[group(tier), :] = e_mv[tier]

    for k in range(1, ntier):
        mat_copy(k, True).wait_recv()
        edge_copy(k, True, e_mat, col_me, s_me, r_me).wait_recv()
    col_halo = halo_copies(col_m.at[0], col_m.at[rows - 1], col_mh, 2)
    halo_start(col_halo)
    narrow = lax.broadcasted_iota(jnp.int32, (levels, cols), 1)
    (ke,) = lookup(col_me[...], (1,))
    ke_low = jnp.where(tier > 0, ke, 0.0)
    ke_high = jnp.where(tier < ntier - 1, ke, 0.0)

    def at_first(edges, r):
        return pltpu.roll(edges, (TILE_COLS - 2 * r) % TILE_COLS, 1)

    def at_last(edges, r):
        return pltpu.roll(edges, TILE_COLS - 2 - 2 * r, 1)

    def widen(block):
        return jnp.concatenate([block] * quarter, axis=1)

    for r in range(rows):
        kx, ky = lookup(col_m[r], (0, 1))
        beside = jnp.where(
            narrow == cols - 1, widen(at_last(ke_high, r)), pltpu.roll(ky, cols - 1, 1)
        )
        cy[r] = face(ky, beside)
        cl[r] = face(ky[:, :TILE_COLS], at_first(ke_low, r))
        if r > 0:
            cx[r] = face(before, kx)
        before = kx
    halo_recv(col_halo)
    for r, side, inside in ((0, 0, has_low), (rows - 1, 1, has_high)):
        (own,) = lookup(col_m[r], (0,))
        (other,) = lookup(col_mh[side], (0,))
        cx[r + side] = face(own, jnp.where(inside, other, 0.0))

    op = a_in[...]
    for r in order:
        for k in range(1, ntier):
            row_copy(r, k, True).wait_recv()
        t1[r] = solve(op, col[r])
    one_halo = halo_copies(t1.at[0], t1.at[rows - 1], halo_1, 3)
    halo_start(one_halo)

    sums = jnp.zeros((ntier, nblk), jnp.float32)
    lines = []
    for t in range(ntier):
        line = t1[0, t * lev : t * lev + 1, :]
        for r in range(1, rows):
            line = line + t1[r, t * lev : t * lev + 1, :]
        lines.append(line)
    lines = jnp.concatenate(lines, axis=0)
    for q in range(quarter):
        part = jnp.sum(lines[:, q * TILE_COLS : (q + 1) * TILE_COLS], axis=1, keepdims=True)
        sums = sums + jnp.where(blkn == labels[0, tier * quarter + q], part, 0.0)
    p2a[0] = jnp.zeros(p2a.shape[1:], jnp.float32)
    p2a[0, 0:ntier, 0:nblk] = sums

    def tier_sum(k):
        return to_tier(p2a.at[0], p2a.at[k], s_pa.at[k], r_pa.at[k], k)

    for k in range(1, ntier):
        tier_sum(k).start()

    for k in range(1, ntier):
        edge_copy(k, True, e_mv, col_e, s_e, r_e).wait_recv()
    edges = solve(op, col_e[...])

    for k in range(1, ntier):
        tier_sum(k).wait_recv()
    acc = p2a[0]
    for k in range(1, ntier):
        acc = acc + p2a[k]
    p2b[0] = acc
    share(p2b, s_pb, r_pb)

    for r in range(rows):
        here = t1[r]
        beside = jnp.where(
            narrow == cols - 1, widen(at_last(edges, r)), pltpu.roll(here, cols - 1, 1)
        )
        flux = cy[r] * (beside - here)
        first = cl[r] * (here[:, :TILE_COLS] - at_first(edges, r))
        mv2[r] = here + (flux - jnp.where(narrow == 0, widen(first), pltpu.roll(flux, 1, 1)))
        if r > 0:
            flow = cx[r] * (here - t1[r - 1])
            mv2[r] -= flow
            mv2[r - 1] += flow

    shared(p2b, r_pb)
    whole = total(p2b)
    power = stat[...] * jnp.exp(fac[...] * whole[0:ntier, 0:nblk] / count)
    mine = lax.broadcasted_iota(jnp.int32, (ntier, nblk), 0) == tier
    pw_out[...] = jnp.sum(jnp.where(mine, power, 0.0), axis=0, keepdims=True)
    gain = []
    for q in range(quarter):
        hit = blkn == labels[0, tier * quarter + q]
        g = jnp.sum(jnp.where(hit, power, 0.0), axis=1, keepdims=True)
        gain.append(jnp.broadcast_to(SOURCE_GAIN * g, (ntier, TILE_COLS)))
    gain = jnp.concatenate(gain, axis=1)
    for r in range(rows):
        for t in range(ntier):
            mv2[r, t * lev : t * lev + 1, :] += gain[t : t + 1, :]

    def finish(r):
        res[r] = solve(op, mv2[r])
        for k in range(1, ntier):
            out_copy(r, k, False).start()
        out[r, :, window(tier)] = res[r, group(tier), :]

    for r in order[:-2]:
        finish(r)
    halo_recv(one_halo)
    for r, side in ((0, 0), (rows - 1, 1)):
        mv2[r] += cx[r + side] * (halo_1[side] - t1[r])
        finish(r)

    for r in order:
        for k in range(1, ntier):
            out_copy(r, k, True).wait_recv()

    for copies in (temp_halo, mat_halo, col_halo, one_halo):
        halo_sent(copies)
    for k in range(1, ntier):
        mat_copy(k, False).wait_send()
        edge_copy(k, False, e_mat, col_me, s_me, r_me).wait_send()
        edge_copy(k, False, e_mv, col_e, s_e, r_e).wait_send()
        tier_sum(k).wait_send()
        for r in range(rows):
            row_copy(r, k, False).wait_send()
            out_copy(r, k, False).wait_send()
    shared(p1, s_p1)
    shared(p2b, s_pb)


def solution(mesh):
    ntier, ntile = mesh.shape["tier"], mesh.shape["tile"]

    def shards(temp, mats, rates, labels, stat, fac, op):
        rows, lev, width = temp.shape
        nblk = stat.shape[1]
        pad = -(-nblk // 128) * 128
        cols, levels = width // ntier, lev * ntier
        f32, i32 = jnp.float32, jnp.int32
        vm = lambda shape, dtype=f32: pltpu.VMEM(shape, dtype)
        dma = pltpu.SemaphoreType.DMA
        vmem = pl.BlockSpec(memory_space=pltpu.VMEM)
        smem = pl.BlockSpec(memory_space=pltpu.SMEM)
        return pl.pallas_call(
            functools.partial(kernel, ntier, ntile, nblk),
            out_shape=(
                jax.ShapeDtypeStruct(temp.shape, f32),
                jax.ShapeDtypeStruct((1, nblk), f32),
            ),
            in_specs=[vmem, vmem, smem, smem, vmem, vmem, vmem],
            out_specs=(vmem, vmem),
            scratch_shapes=[
                vm((2, lev, width)), vm((2, lev, width), i32), vm((rows, lev, width)),
                vm((ntier, lev, TILE_COLS), i32), vm((ntier, lev, TILE_COLS)),
                vm((rows, levels, cols), i32), vm((levels, TILE_COLS), i32),
                vm((2, levels, cols), i32),
                vm((rows, levels, cols)), vm((levels, TILE_COLS)), vm((rows, levels, cols)),
                vm((2, levels, cols)), vm((rows, levels, cols)), vm((rows, levels, cols)),
                vm((rows + 1, levels, cols)), vm((rows, levels, cols)),
                vm((rows, levels, TILE_COLS)),
                vm((ntile, 8, pad)), vm((ntier, 8, pad)), vm((ntile, 8, pad)),
                dma((4, 2)), dma((4, 2)), dma((rows, ntier)), dma((rows, ntier)),
                dma((ntier,)), dma((ntier,)), dma((ntier,)), dma((ntier,)),
                dma((ntier,)), dma((ntier,)), dma((rows, ntier)), dma((rows, ntier)),
                dma, dma, dma((ntier,)), dma((ntier,)), dma, dma,
            ],
            compiler_params=pltpu.CompilerParams(
                collective_id=0, has_side_effects=True, vmem_limit_bytes=40 * 1024 * 1024
            ),
        )(temp, mats, rates, labels, stat, fac, op)

    return jax.shard_map(
        shards,
        mesh=mesh,
        in_specs=(P("tile", "tier", None), P("tile", "tier", None), P(), P("tile", None), P(), P(), P()),
        out_specs=(P("tile", "tier", None), P("tier", None)),
        check_vma=False,
    )
```

time: 145 us -> 44.1 us (0.30); the launches traced: 142 us -> 43.7 us
  blocking collectives: 79.4 us -> 0 us
  Pallas kernels: 0 us -> 36.3 us
  other arithmetic: 19.3 us -> 0 us
  starting transfers between devices: 17.9 us -> 0 us
  local copies, waits for them, and re-layouts: 21 us -> 6.74 us
  waiting for transfers between devices: 2.13 us -> 0 us
  matrix products: 1.71 us -> 0 us
    psum x2 -> x0, blocking collectives: 39.9 us -> none  [leak_tiers(): block_sum, block_count = lax.psum((partial_value[0], counts), 'tile')]
    all_to_all x4 -> x0, blocking collectives: 39.5 us -> none  [the longest x2 19.8 us: shards(): lax.all_to_all(moved_field, 'tier', split_axis=2, concat_axis=1, tiled=True)]
    pallas_call x0 -> x1, Pallas kernels: none -> 36.3 us  [shards(): pl.pallas_call(functools.partial(kernel, ntier, ntile, nblk), out_shape=(...]
    ppermute x6 -> x0, starting transfers between devices: 17.9 us -> none  [the longest x3 14 us: extended(): lax.ppermute(lax.slice_in_dim(block, block.shape[dim] - width, None, axis...]
    select_n x2 -> x0, other arithmetic: 11.9 us -> none  [the longest x1 6.55 us: lookup_codes(): jnp.where(is_material, material_transport_rates[1, material], stacking_co...]
    unnamed x20 -> x16, local copies, waits for them, and re-layouts: 11.4 us -> 6.74 us
    all_to_all x7 -> x0, local copies, waits for them, and re-layouts: 3.72 us -> none  [the longest x3 2.06 us: shards(): lax.all_to_all(moved_field, 'tier', split_axis=2, concat_axis=1, tiled=True)]
    all_to_all x2 -> x0, other arithmetic: 3.46 us -> none  [shards(): lax.all_to_all(moved_field, 'tier', split_axis=2, concat_axis=1, tiled=True)]
  transfers between devices with their start and end apart: 6 -> 0, of which waited for: 2 -> 0; matrix products, arithmetic and copies ran while one was open for 10% -> 0% of each run, Pallas kernels for 0% -> 0%
where the time goes in v1:
time: 44.1 us; the launch traced here: 43.7 us
  Pallas kernels  36.3 us (82%)
  local copies, waits for them, and re-layouts  6.74 us (15%)
  between operations  0.66 us (1%)
    pallas_call x1, Pallas kernels, shards(): pl.pallas_call(functools.partial(kernel, ntier, ntile, nblk), out_shape=(...  36.3 us
    unnamed x16, local copies, waits for them, and re-layouts  6.74 us

profile of v1, /device:TPU:0, one launch (start us, length us, event | category | flops | bytes accessed | tf_op | source)
XLA Modules:
  0.0 43.7 jit_solution(2402658570161189460)
XLA Ops:
  0.6 0.0 copy-start
  0.6 1.0 %copy-done = f32[4,24,1024]{2,1,0:T(8,128)S(1)} copy-done((f32[4,24,1024]{2,1,0:T(8,128)S(1)}, f32[4,24,1024]{2,1,0:T(8,128)}, u32[]{:S(2)}) %copy-start) | copy-done | bytes 393240
  1.6 0.0 copy-start.1
  1.6 1.0 %copy-done.1 = s32[4,24,1024]{2,1,0:T(8,128)S(1)} copy-done((s32[4,24,1024]{2,1,0:T(8,128)S(1)}, s32[4,24,1024]{2,1,0:T(8,128)}, u32[]{:S(2)}) %copy-start.1) | copy-done | bytes 393240
  2.6 0.0 copy-start.2
  2.6 0.8 %copy-done.2 = f32[96,96]{1,0:T(8,128)S(1)} copy-done((f32[96,96]{1,0:T(8,128)S(1)}, f32[96,96]{1,0:T(8,128)}, u32[]{:S(2)}) %copy-start.2) | copy-done | bytes 36888
  3.4 0.0 copy-start.3
  3.4 0.7 %copy-done.3 = f32[4,16]{1,0:T(4,128)S(1)} copy-done((f32[4,16]{1,0:T(4,128)S(1)}, f32[4,16]{1,0:T(4,128)}, u32[]{:S(2)}) %copy-start.3) | copy-done | bytes 280
  4.1 0.0 copy-start.4
  4.1 0.7 %copy-done.4 = f32[4,16]{1,0:T(4,128)S(1)} copy-done((f32[4,16]{1,0:T(4,128)S(1)}, f32[4,16]{1,0:T(4,128)}, u32[]{:S(2)}) %copy-start.4) | copy-done | bytes 280
  4.8 0.0 copy-start.5
  4.8 0.7 %copy-done.5 = f32[2,8]{1,0:T(2,128)S(1)} copy-done((f32[2,8]{1,0:T(2,128)S(1)}, f32[2,8]{1,0:T(2,128)}, u32[]{:S(2)}) %copy-start.5) | copy-done | bytes 88
  5.5 0.0 copy-start.6
  5.5 0.7 %copy-done.6 = s32[1,8]{1,0:T(1,128)S(1)} copy-done((s32[1,8]{1,0:T(1,128)S(1)}, s32[1,8]{1,0:T(1,128)}, u32[]{:S(2)}) %copy-start.6) | copy-done | bytes 56
  6.1 36.3 %shard_map.86 = (f32[4,24,1024]{2,1,0:T(8,128)S(1)}, f32[1,16]{1,0:T(1,128)S(1)}) custom-call(f32[4,24,1024]{2,1,0:T(8,128)S(1)} %copy-done, s32[4,24,1024]{2,1,0:T(8,128)S(1)} %copy-done.1, f32[2,8]{1,0:T(2,128)S(1)} %copy-done.5, s32[1,8]{1,0:T(1,128)S(1)} %copy-done.6, f32[4,16]{1,0:T(4,128)S(1)} %copy-done.3, f32[4,16]{1,0:T(4,128)S(1)} %copy-done.4, ...), custom_call_target="tpu_custom_call" | custom-call | tf_op jit(solution)/shard_map/pallas_call | solution.py:409
  42.5 0.7 %copy.11 = f32[4,24,1024]{2,1,0:T(8,128)} copy(f32[4,24,1024]{2,1,0:T(8,128)S(1)} %get-tuple-element.4) | data formatting | bytes 786432
  43.2 0.5 %copy.12 = f32[1,16]{1,0:T(1,128)} copy(f32[1,16]{1,0:T(1,128)S(1)} %get-tuple-element.5) | data formatting | bytes 128
Async XLA Ops:
  0.6 1.0 %copy-start = (f32[4,24,1024]{2,1,0:T(8,128)S(1)}, f32[4,24,1024]{2,1,0:T(8,128)}, u32[]{:S(2)}) copy-start(f32[4,24,1024]{2,1,0:T(8,128)} %t_in.1) | copy-start | bytes 1179652
  1.6 1.0 %copy-start.1 = (s32[4,24,1024]{2,1,0:T(8,128)S(1)}, s32[4,24,1024]{2,1,0:T(8,128)}, u32[]{:S(2)}) copy-start(s32[4,24,1024]{2,1,0:T(8,128)} %m_in.1) | copy-start | bytes 1179652
  2.6 0.8 %copy-start.2 = (f32[96,96]{1,0:T(8,128)S(1)}, f32[96,96]{1,0:T(8,128)}, u32[]{:S(2)}) copy-start(f32[96,96]{1,0:T(8,128)} %a_in.1) | copy-start | bytes 110596
  3.4 0.7 %copy-start.3 = (f32[4,16]{1,0:T(4,128)S(1)}, f32[4,16]{1,0:T(4,128)}, u32[]{:S(2)}) copy-start(f32[4,16]{1,0:T(4,128)} %stat.1) | copy-start | bytes 772
  4.1 0.7 %copy-start.4 = (f32[4,16]{1,0:T(4,128)S(1)}, f32[4,16]{1,0:T(4,128)}, u32[]{:S(2)}) copy-start(f32[4,16]{1,0:T(4,128)} %fac.1) | copy-start | bytes 772
  4.8 0.7 %copy-start.5 = (f32[2,8]{1,0:T(2,128)S(1)}, f32[2,8]{1,0:T(2,128)}, u32[]{:S(2)}) copy-start(f32[2,8]{1,0:T(2,128)} %rates.1) | copy-start | bytes 196
  5.5 0.7 %copy-start.6 = (s32[1,8]{1,0:T(1,128)S(1)}, s32[1,8]{1,0:T(1,128)}, u32[]{:S(2)}) copy-start(s32[1,8]{1,0:T(1,128)} %labels.1) | copy-start | bytes 100

commit v2 on v1

--- a/solution.py
+++ b/solution.py
@@ -23,8 +23,9 @@
 
 def kernel(
     ntier, ntile, nblk,
-    t_in, m_in, rates, labels, stat, fac, a_in,
+    t_hbm, m_hbm, rates_hbm, labels_hbm, stat_hbm, fac_hbm, a_hbm,
     out, pw_out,
+    t_in, m_in, rates, labels, stat, fac, a_in, s_in,
     halo_t, halo_m, mv, e_mat, e_mv, col_m, col_me, col_mh, col, col_e, t1, halo_1, mv2, res,
     cx, cy, cl, p1, p2a, p2b,
     s_halo, r_halo, s_a2a, r_a2a, s_mat, r_mat, s_me, r_me, s_e, r_e, s_out, r_out,
@@ -39,6 +40,16 @@
     nmat = rates.shape[1]
     order = [r for r in range(1, rows - 1)] + [0, rows - 1]
 
+    loads = [
+        pltpu.make_async_copy(src, dst, s_in.at[i])
+        for i, (src, dst) in enumerate(
+            ((t_hbm, t_in), (m_hbm, m_in), (labels_hbm, labels), (rates_hbm, rates),
+             (stat_hbm, stat), (fac_hbm, fac), (a_hbm, a_in))
+        )
+    ]
+    for load in loads:
+        load.start()
+
     def tier_at(k):
         return lax.rem(tier + k, ntier)
 
@@ -88,6 +99,8 @@
     blk1 = lax.broadcasted_iota(jnp.int32, (1, nblk), 1)
     blkn = lax.broadcasted_iota(jnp.int32, (ntier, nblk), 1)
 
+    for load in loads:
+        load.wait()
     sums = jnp.zeros((1, nblk), jnp.float32)
     areas = jnp.zeros((1, nblk), jnp.float32)
     active = t_in[0, 0:1, :]
@@ -101,7 +114,6 @@
     p1[0] = jnp.zeros(p1.shape[1:], jnp.float32)
     p1[0, 0:1, 0:nblk] = sums
     p1[0, 1:2, 0:nblk] = areas
-    pack_edges(m_in, e_mat)
 
     pl.semaphore_wait(barrier, ntier - 1 + ntile - 1)
 
@@ -166,8 +178,8 @@
         halo_1[1] = jnp.zeros(halo_1.shape[1:], jnp.float32)
         col_mh[1] = jnp.zeros(col_mh.shape[1:], jnp.int32)
 
-    temp_halo = halo_copies(t_in.at[0], t_in.at[rows - 1], halo_t, 0)
-    mat_halo = halo_copies(m_in.at[0], m_in.at[rows - 1], halo_m, 1)
+    temp_halo = halo_copies(t_hbm.at[0], t_hbm.at[rows - 1], halo_t, 0)
+    mat_halo = halo_copies(m_hbm.at[0], m_hbm.at[rows - 1], halo_m, 1)
     halo_start(temp_halo)
     halo_start(mat_halo)
 
@@ -180,7 +192,7 @@
     def mat_copy(k, receive):
         src = tier_at(ntier - k) if receive else tier
         return to_tier(
-            m_in.at[:, :, window(tier_at(k))], col_m.at[:, group(src), :],
+            m_hbm.at[:, :, window(tier_at(k))], col_m.at[:, group(src), :],
             s_mat.at[k], r_mat.at[k], k,
         )
 
@@ -206,6 +218,8 @@
 
     for k in range(1, ntier):
         mat_copy(k, False).start()
+    pack_edges(m_in, e_mat)
+    for k in range(1, ntier):
         edge_copy(k, False, e_mat, col_me, s_me, r_me).start()
     col_m[:, group(tier), :] = m_in[:, :, window(tier)]
     col_me[group(tier), :] = e_mat[tier]
@@ -405,16 +419,18 @@
         vm = lambda shape, dtype=f32: pltpu.VMEM(shape, dtype)
         dma = pltpu.SemaphoreType.DMA
         vmem = pl.BlockSpec(memory_space=pltpu.VMEM)
-        smem = pl.BlockSpec(memory_space=pltpu.SMEM)
         return pl.pallas_call(
             functools.partial(kernel, ntier, ntile, nblk),
             out_shape=(
                 jax.ShapeDtypeStruct(temp.shape, f32),
                 jax.ShapeDtypeStruct((1, nblk), f32),
             ),
-            in_specs=[vmem, vmem, smem, smem, vmem, vmem, vmem],
+            in_specs=[pl.BlockSpec(memory_space=pltpu.HBM)] * 7,
             out_specs=(vmem, vmem),
             scratch_shapes=[
+                vm(temp.shape), vm(mats.shape, i32), pltpu.SMEM(rates.shape, f32),
+                pltpu.SMEM(labels.shape, i32), vm(stat.shape), vm(fac.shape), vm(op.shape),
+                dma((7,)),
                 vm((2, lev, width)), vm((2, lev, width), i32), vm((rows, lev, width)),
                 vm((ntier, lev, TILE_COLS), i32), vm((ntier, lev, TILE_COLS)),
                 vm((rows, levels, cols), i32), vm((levels, TILE_COLS), i32),
@@ -430,7 +446,7 @@
                 dma, dma, dma((ntier,)), dma((ntier,)), dma, dma,
             ],
             compiler_params=pltpu.CompilerParams(
-                collective_id=0, has_side_effects=True, vmem_limit_bytes=40 * 1024 * 1024
+                collective_id=0, has_side_effects=True, vmem_limit_bytes=62 * 1024 * 1024
             ),
         )(temp, mats, rates, labels, stat, fac, op)
 

time: 44.1 us -> 39.9 us (0.905)
  local copies, waits for them, and re-layouts: 6.74 us -> 2.28 us
  Pallas kernels: 36.3 us -> 36.8 us
    unnamed x16 -> x4, local copies, waits for them, and re-layouts: 6.74 us -> 2.28 us
    pallas_call x1, Pallas kernels: 36.3 us -> 36.8 us  [shards(): pl.pallas_call(functools.partial(kernel, ntier, ntile, nblk), out_shape=(...]
where the time goes in v2:
time: 39.9 us; the launch traced here: 39.8 us
  Pallas kernels  36.8 us (92%)
  local copies, waits for them, and re-layouts  2.28 us (6%)
  between operations  0.65 us (2%)
    pallas_call x1, Pallas kernels, shards(): pl.pallas_call(functools.partial(kernel, ntier, ntile, nblk), out_shape=(...  36.8 us
    unnamed x4, local copies, waits for them, and re-layouts  2.28 us

profile of v2, /device:TPU:0, one launch (start us, length us, event | category | flops | bytes accessed | tf_op | source)
XLA Modules:
  0.0 39.8 jit_solution(7804165175597438360)
XLA Ops:
  0.6 36.8 %shard_map.86 = (f32[4,24,1024]{2,1,0:T(8,128)}, f32[1,16]{1,0:T(1,128)}) custom-call(f32[4,24,1024]{2,1,0:T(8,128)} %t_hbm.1, s32[4,24,1024]{2,1,0:T(8,128)} %m_hbm.1, f32[2,8]{1,0:T(2,128)} %rates_hbm.1, s32[1,8]{1,0:T(1,128)} %labels_hbm.1, f32[4,16]{1,0:T(4,128)} %stat_hbm.1, f32[4,16]{1,0:T(4,128)} %fac_hbm.1, f32[96,96]{1,0:T(8,128)} %a_hbm.1), custom_call_target="tpu_custom_call" | custom-call | tf_op jit(solution)/shard_map/pallas_call | solution.py:422
  37.5 0.0 copy-start
  37.5 1.8 %copy.11 = f32[4,24,1024]{2,1,0:T(8,128)} copy(f32[4,24,1024]{2,1,0:T(8,128)} %get-tuple-element.4) | data formatting | bytes 786432
  39.2 0.0 copy-done
  39.3 0.5 %copy.12 = f32[1,16]{1,0:T(1,128)} copy(f32[1,16]{1,0:T(1,128)S(1)} %copy-done) | data formatting | bytes 128
Async XLA Ops:
  37.5 1.8 %copy-start = (f32[1,16]{1,0:T(1,128)S(1)}, f32[1,16]{1,0:T(1,128)}, u32[]{:S(2)}) copy-start(f32[1,16]{1,0:T(1,128)} %get-tuple-element.5) | copy-start | bytes 196

commit v3 on v2

--- a/solution.py
+++ b/solution.py
@@ -27,7 +27,7 @@
     out, pw_out,
     t_in, m_in, rates, labels, stat, fac, a_in, s_in,
     halo_t, halo_m, mv, e_mat, e_mv, col_m, col_me, col_mh, col, col_e, t1, halo_1, mv2, res,
-    cx, cy, cl, p1, p2a, p2b,
+    cx, cy, cl, by_block, p1, p2a, p2b,
     s_halo, r_halo, s_a2a, r_a2a, s_mat, r_mat, s_me, r_me, s_e, r_e, s_out, r_out,
     s_p1, r_p1, s_pa, r_pa, s_pb, r_pb,
 ):
@@ -273,6 +273,33 @@
         edge_copy(k, False, e_mv, col_e, s_e, r_e).start()
     col_e[group(tier), :] = e_mv[tier]
 
+    level_sums = mv[0] + mv[1]
+    for r in range(2, rows):
+        level_sums = level_sums + mv[r]
+    blkl = lax.broadcasted_iota(jnp.int32, (lev, nblk), 1)
+    sums = jnp.zeros((lev, nblk), jnp.float32)
+    for j in range(width // TILE_COLS):
+        part = jnp.sum(
+            level_sums[:, j * TILE_COLS : (j + 1) * TILE_COLS], axis=1, keepdims=True
+        )
+        sums = sums + jnp.where(blkl == labels[0, j], part, 0.0)
+    by_block[...] = jnp.zeros_like(by_block)
+    by_block[group(tier), :] = sums
+    op = a_in[...]
+    active_rows = jnp.concatenate(
+        [op[t * lev : t * lev + 1, :] for t in range(ntier)]
+        + [jnp.zeros((8 - ntier, levels), jnp.float32)],
+        axis=0,
+    )
+    p2a[0] = jnp.zeros(p2a.shape[1:], jnp.float32)
+    p2a[0, :, 0:nblk] = solve(active_rows, by_block[...])
+
+    def tier_sum(k):
+        return to_tier(p2a.at[0], p2a.at[k], s_pa.at[k], r_pa.at[k], k)
+
+    for k in range(1, ntier):
+        tier_sum(k).start()
+
     for k in range(1, ntier):
         mat_copy(k, True).wait_recv()
         edge_copy(k, True, e_mat, col_me, s_me, r_me).wait_recv()
@@ -302,13 +329,14 @@
         if r > 0:
             cx[r] = face(before, kx)
         before = kx
-    halo_recv(col_halo)
-    for r, side, inside in ((0, 0, has_low), (rows - 1, 1, has_high)):
-        (own,) = lookup(col_m[r], (0,))
-        (other,) = lookup(col_mh[side], (0,))
-        cx[r + side] = face(own, jnp.where(inside, other, 0.0))
-
-    op = a_in[...]
+    for k in range(1, ntier):
+        tier_sum(k).wait_recv()
+    acc = p2a[0]
+    for k in range(1, ntier):
+        acc = acc + p2a[k]
+    p2b[0] = acc
+    share(p2b, s_pb, r_pb)
+
     for r in order:
         for k in range(1, ntier):
             row_copy(r, k, True).wait_recv()
@@ -316,37 +344,9 @@
     one_halo = halo_copies(t1.at[0], t1.at[rows - 1], halo_1, 3)
     halo_start(one_halo)
 
-    sums = jnp.zeros((ntier, nblk), jnp.float32)
-    lines = []
-    for t in range(ntier):
-        line = t1[0, t * lev : t * lev + 1, :]
-        for r in range(1, rows):
-            line = line + t1[r, t * lev : t * lev + 1, :]
-        lines.append(line)
-    lines = jnp.concatenate(lines, axis=0)
-    for q in range(quarter):
-        part = jnp.sum(lines[:, q * TILE_COLS : (q + 1) * TILE_COLS], axis=1, keepdims=True)
-        sums = sums + jnp.where(blkn == labels[0, tier * quarter + q], part, 0.0)
-    p2a[0] = jnp.zeros(p2a.shape[1:], jnp.float32)
-    p2a[0, 0:ntier, 0:nblk] = sums
-
-    def tier_sum(k):
-        return to_tier(p2a.at[0], p2a.at[k], s_pa.at[k], r_pa.at[k], k)
-
-    for k in range(1, ntier):
-        tier_sum(k).start()
-
     for k in range(1, ntier):
         edge_copy(k, True, e_mv, col_e, s_e, r_e).wait_recv()
     edges = solve(op, col_e[...])
-
-    for k in range(1, ntier):
-        tier_sum(k).wait_recv()
-    acc = p2a[0]
-    for k in range(1, ntier):
-        acc = acc + p2a[k]
-    p2b[0] = acc
-    share(p2b, s_pb, r_pb)
 
     for r in range(rows):
         here = t1[r]
@@ -384,6 +384,11 @@
 
     for r in order[:-2]:
         finish(r)
+    halo_recv(col_halo)
+    for r, side, inside in ((0, 0, has_low), (rows - 1, 1, has_high)):
+        (own,) = lookup(col_m[r], (0,))
+        (other,) = lookup(col_mh[side], (0,))
+        cx[r + side] = face(own, jnp.where(inside, other, 0.0))
     halo_recv(one_halo)
     for r, side in ((0, 0), (rows - 1, 1)):
         mv2[r] += cx[r + side] * (halo_1[side] - t1[r])
@@ -439,7 +444,7 @@
                 vm((2, levels, cols)), vm((rows, levels, cols)), vm((rows, levels, cols)),
                 vm((rows + 1, levels, cols)), vm((rows, levels, cols)),
                 vm((rows, levels, TILE_COLS)),
-                vm((ntile, 8, pad)), vm((ntier, 8, pad)), vm((ntile, 8, pad)),
+                vm((levels, nblk)), vm((ntile, 8, pad)), vm((ntier, 8, pad)), vm((ntile, 8, pad)),
                 dma((4, 2)), dma((4, 2)), dma((rows, ntier)), dma((rows, ntier)),
                 dma((ntier,)), dma((ntier,)), dma((ntier,)), dma((ntier,)),
                 dma((ntier,)), dma((ntier,)), dma((rows, ntier)), dma((rows, ntier)),

time: 39.9 us -> 35.2 us (0.88)
  Pallas kernels: 36.8 us -> 32.1 us
    pallas_call x1, Pallas kernels: 36.8 us -> 32.1 us  [shards(): pl.pallas_call(functools.partial(kernel, ntier, ntile, nblk), out_shape=(...]
where the time goes in v3:
time: 35.2 us; the launch traced here: 35 us
  Pallas kernels  32.1 us (91%)
  local copies, waits for them, and re-layouts  2.28 us (6%)
  between operations  0.65 us (2%)
    pallas_call x1, Pallas kernels, shards(): pl.pallas_call(functools.partial(kernel, ntier, ntile, nblk), out_shape=(...  32.1 us
    unnamed x4, local copies, waits for them, and re-layouts  2.28 us

profile of v3, /device:TPU:0, one launch (start us, length us, event | category | flops | bytes accessed | tf_op | source)
XLA Modules:
  0.0 35.0 jit_solution(15889908747206125200)
XLA Ops:
  0.6 32.1 %shard_map.86 = (f32[4,24,1024]{2,1,0:T(8,128)}, f32[1,16]{1,0:T(1,128)}) custom-call(f32[4,24,1024]{2,1,0:T(8,128)} %t_hbm.1, s32[4,24,1024]{2,1,0:T(8,128)} %m_hbm.1, f32[2,8]{1,0:T(2,128)} %rates_hbm.1, s32[1,8]{1,0:T(1,128)} %labels_hbm.1, f32[4,16]{1,0:T(4,128)} %stat_hbm.1, f32[4,16]{1,0:T(4,128)} %fac_hbm.1, f32[96,96]{1,0:T(8,128)} %a_hbm.1), custom_call_target="tpu_custom_call" | custom-call | tf_op jit(solution)/shard_map/pallas_call | solution.py:427
  32.7 0.0 copy-start
  32.7 1.8 %copy.11 = f32[4,24,1024]{2,1,0:T(8,128)} copy(f32[4,24,1024]{2,1,0:T(8,128)} %get-tuple-element.4) | data formatting | bytes 786432
  34.5 0.0 copy-done
  34.5 0.5 %copy.12 = f32[1,16]{1,0:T(1,128)} copy(f32[1,16]{1,0:T(1,128)S(1)} %copy-done) | data formatting | bytes 128
Async XLA Ops:
  32.7 1.8 %copy-start = (f32[1,16]{1,0:T(1,128)S(1)}, f32[1,16]{1,0:T(1,128)}, u32[]{:S(2)}) copy-start(f32[1,16]{1,0:T(1,128)} %get-tuple-element.5) | copy-start | bytes 196
